TPU v7x, 32 devices: a whole 2x2x4 slice. The times are simulated.
32 devices in a mesh: row: 2 (over x), col: 4 (over z), depth: 4 (over y, core).
Axes of the slice: x: 2, y: 2, z: 4, core: 2. Of those that a mesh axis runs over, the one named last changes fastest.
Arguments:
- tokens: bfloat16 [256, 8192], P(('col', 'depth'), 'row'), may hold values from -6 to 6
- gate_weight: bfloat16 [8192, 14336], P('row', ('col', 'depth')), may hold values from -0.109375 to 0.109375
- up_weight: bfloat16 [8192, 14336], P('row', ('col', 'depth')), may hold values from -0.109375 to 0.109375
- down_weight: bfloat16 [14336, 8192], P(('col', 'depth'), 'row'), may hold values from -0.078125 to 0.078125
- gate_mask: int32 [64, 112], P('row', ('col', 'depth')), may hold values 0 or 1
- up_mask: int32 [64, 112], P('row', ('col', 'depth')), may hold values 0 or 1
- down_mask: int32 [112, 64], P(('col', 'depth'), 'row'), may hold values 0 or 1
- grad_out: bfloat16 [256, 8192], P(('col', 'depth'), 'row'), may hold values from -1.5 to 1.5
Outputs:
- mixed: bfloat16 [256, 8192], P(('col', 'depth'), 'row')
- grad_tokens: bfloat16 [256, 8192], P(('col', 'depth'), 'row')
- grad_gate_weight: bfloat16 [8192, 14336], P('row', ('col', 'depth'))
- grad_up_weight: bfloat16 [8192, 14336], P('row', ('col', 'depth'))
- grad_down_weight: bfloat16 [14336, 8192], P(('col', 'depth'), 'row')
Inputs may be any that keep to these rules, and one draw needn't show every extreme that they name: `gate_mask`: 1 keeps the 128 x 128 block of the gate projection, 0 zeroes it. `up_mask`: 1 keeps the 128 x 128 block of the up projection, 0 zeroes it. `down_mask`: 1 keeps the 128 x 128 block of the down projection, 0 zeroes it.
All inputs are finite; a program needn't handle non-finite values.
Results may differ from a plain program's by a relative error of at most 0.015.
Values may be sent and summed in bfloat16 or wider, within the bound.
A program may use at most 128 MiB of HBM per device.

v0:
```python
import jax
import jax.numpy as jnp
from jax import lax
from jax.sharding import PartitionSpec as P

BLK = 128


def expand(mask):
    return jnp.repeat(jnp.repeat(mask, BLK, axis=0), BLK, axis=1) > 0


def swiglu(sums):
    width = sums.shape[1] // 2
    gate = sums[:, :width]
    up = sums[:, width:]
    sig = jax.nn.sigmoid(gate)
    return (gate * sig * up).astype(jnp.bfloat16)


def swiglu_back(sums, grad_act):
    width = sums.shape[1] // 2
    gate = sums[:, :width]
    up = sums[:, width:]
    sig = jax.nn.sigmoid(gate)
    grad_gate = grad_act * up * sig * (1.0 + gate * (1.0 - sig))
    grad_up = grad_act * gate * sig
    return jnp.concatenate([grad_gate, grad_up], axis=1).astype(jnp.bfloat16)


def row_sums(term, rows):
    return lax.psum_scatter(
        term(jnp.int32(0), lax.axis_size("row") * rows), "row", scatter_dimension=0, tiled=True
    )


def row_gather(block):
    return lax.all_gather(block, "row", axis=0, tiled=True)


def group_sums(term, rows):
    return lax.psum_scatter(
        term(jnp.int32(0), rows * lax.axis_size(("col", "depth"))).astype(jnp.bfloat16),
        ("col", "depth"),
        scatter_dimension=0,
        tiled=True,
    ).astype(jnp.float32)


def local(tokens, gate_weight, up_weight, down_weight, gate_mask, up_mask, down_mask, grad_out):
    zero_value = jnp.zeros((), jnp.bfloat16)
    keep_gate = expand(gate_mask)
    keep_up = expand(up_mask)
    keep_down = expand(down_mask)
    w_both = jnp.concatenate(
        [jnp.where(keep_gate, gate_weight, zero_value), jnp.where(keep_up, up_weight, zero_value)],
        axis=1,
    )
    w_down = jnp.where(keep_down, down_weight, zero_value)
    x_all, grad_all = (
        lax.all_gather(tokens, ("col", "depth"), axis=0, tiled=True),
        lax.all_gather(grad_out, ("col", "depth"), axis=0, tiled=True),
    )
    total = x_all.shape[0]
    split_rows = total // lax.axis_size("row")
    own_rows = tokens.shape[0]
    inner = (((0,), (0,)), ((), ()))
    outer = (((1,), (1,)), ((), ()))

    def hidden_term(start, count):
        return jnp.dot(x_all, w_both, preferred_element_type=jnp.float32)

    def act_term(start, count):
        return lax.dot_general(grad_all, w_down, outer, preferred_element_type=jnp.float32)

    sums = row_sums(hidden_term, split_rows)
    act_all = row_gather(swiglu(sums))

    def out_term(start, count):
        return jnp.dot(act_all, w_down, preferred_element_type=jnp.float32)

    mixed = group_sums(out_term, own_rows).astype(jnp.bfloat16)
    grad_down = lax.dot_general(act_all, grad_all, inner, preferred_element_type=jnp.float32)
    grad_down_weight = jnp.where(keep_down, grad_down, jnp.float32(0.0)).astype(jnp.bfloat16)
    grad_act = row_sums(act_term, split_rows)
    grads_all = row_gather(swiglu_back(sums, grad_act))
    grad_both = lax.dot_general(x_all, grads_all, inner, preferred_element_type=jnp.float32)
    width = grad_both.shape[1] // 2
    grad_gate_weight = jnp.where(keep_gate, grad_both[:, :width], jnp.float32(0.0)).astype(
        jnp.bfloat16
    )
    grad_up_weight = jnp.where(keep_up, grad_both[:, width:], jnp.float32(0.0)).astype(jnp.bfloat16)

    def input_term(start, count):
        return lax.dot_general(grads_all, w_both, outer, preferred_element_type=jnp.float32)

    grad_tokens = group_sums(input_term, own_rows).astype(jnp.bfloat16)
    return (mixed, grad_tokens, grad_gate_weight, grad_up_weight, grad_down_weight)


def solution(mesh):
    return jax.shard_map(
        local,
        mesh=mesh,
        in_specs=(
            P(("col", "depth"), "row"),
            P("row", ("col", "depth")),
            P("row", ("col", "depth")),
            P(("col", "depth"), "row"),
            P("row", ("col", "depth")),
            P("row", ("col", "depth")),
            P(("col", "depth"), "row"),
            P(("col", "depth"), "row"),
        ),
        out_specs=(
            P(("col", "depth"), "row"),
            P(("col", "depth"), "row"),
            P("row", ("col", "depth")),
            P("row", ("col", "depth")),
            P(("col", "depth"), "row"),
        ),
        check_vma=False,
    )
```

profile of v0, /device:TPU:0, one launch (start us, length us, event | category | flops | bytes accessed | tf_op | source)
XLA Modules:
  0.0 305.2 jit_solution(14030705559243978038)
XLA Ops:
  7.2 0.0 all-gather.5.cloned.1.call-start
  7.2 0.7 all-gather.5.cloned.1.call-update
  7.9 0.0 all-gather.3.cloned.1.call-start
  7.9 0.7 all-gather.3.cloned.1.call-update
  8.6 0.0 reduce-scatter.9.cloned.1.call-start
  8.7 0.7 broadcast_compare_fusion.1
  9.4 0.1 broadcast_bitcast_fusion
  9.5 0.7 broadcast_compare_fusion
  10.2 44.1 %all-gather.5.cloned.1.call-done = bf16[256,4096]{1,0:T(8,128)(2,1)} async-done(((bf16[16,4096]{1,0:T(8,128)(2,1)}), bf16[256,4096]{1,0:T(8,128)(2,1)}) %all-gather.5.cloned.1.call-update) | async-done | bytes 2097168 | tf_op jit(solution)/shard_map/all_gather | solution.py:62
  54.3 5.1 %broadcast_in_dim.42 = pred[896,32,128]{2,1,0:T(32,128)(4,1)S(1)} broadcast(pred[896,32]{1,0:T(8,128)(4,1)S(1)} %bitcast.50), dimensions={0,1} | broadcast | bytes 3698688 | tf_op jit(solution)/shard_map/broadcast_in_dim | solution.py:10
  59.5 0.0 copy-start
  59.5 1.8 copy-done
  61.3 0.0 copy-start.2
  61.3 7.9 %fusion.9 = f32[256,896]{0,1:T(8,128)} fusion(bf16[256,4096]{1,0:T(8,128)(2,1)} %all-gather.5.cloned.1.call-done, bf16[896,4096]{1,0:T(8,128)(2,1)} %param.11, pred[112,8,32,128]{3,2,1,0:T(32,128)(4,1)S(1)} %bitcast.47), kind=kOutput, calls=%fused_computation.18 | convolution fusion | flops 1882718208 | bytes 14024704 | tf_op jit(solution)/shard_map/dot_general | solution.py:74
  69.2 0.0 reduce-scatter.9.cloned.1.call-update
  69.2 0.0 reduce-scatter.5.cloned.1.call-start
  69.2 0.0 copy-done.2
  69.3 0.1 broadcast_bitcast_fusion.1
  69.4 10.8 %copy.13 = bf16[4096,896]{0,1:T(8,128)(2,1)} copy(bf16[4096,896]{1,0:T(8,128)(2,1)} %param.9) | data formatting | bytes 14680064 | tf_op args[1]
  80.2 10.8 %copy.14 = bf16[4096,896]{0,1:T(8,128)(2,1)} copy(bf16[4096,896]{1,0:T(8,128)(2,1)} %param.10) | data formatting | bytes 14680064 | tf_op args[2]
  91.0 10.5 %bitcast_select_fusion.1 = (bf16[4096,896]{0,1:T(8,128)(2,1)}, bf16[4096,896]{0,1:T(8,128)(2,1)}) fusion(bf16[4096,896]{0,1:T(8,128)(2,1)} %copy.14, pred[4096,7]{0,1:T(8,128)(4,1)S(1)} %bitcast.51, bf16[4096,896]{0,1:T(8,128)(2,1)} %copy.13, pred[4096,7]{0,1:T(8,128)(4,1)S(1)} %bitcast.53), kind=kLoop, calls=%fused_computation.1 | loop fusion | flops 7340032 | bytes 29417472 | tf_op jit(solution)/shard_map/jit(_where)/select_n | solution.py:56
  101.5 0.0 all-gather.3.cloned.1.call-done
  101.5 11.4 %fusion.8 = f32[256,1792]{0,1:T(8,128)} fusion(bf16[256,4096]{1,0:T(8,128)(2,1)} %all-gather.3.cloned.1.call-done, bf16[4096,896]{0,1:T(8,128)(2,1)} %get-tuple-element.15, bf16[4096,896]{0,1:T(8,128)(2,1)} %get-tuple-element.16), kind=kOutput, calls=%fused_computation.17 | convolution fusion | flops 3787456512 | bytes 18612224 | tf_op jit(solution)/shard_map/dot_general | solution.py:71
  113.0 0.0 reduce-scatter.5.cloned.1.call-update
  113.0 0.0 reduce-scatter.11.cloned.1.call-start
  113.0 3.5 %reduce-scatter.9.cloned.1.call-done = f32[128,896]{0,1:T(8,128)} async-done(((f32[256,896]{0,1:T(8,128)}), f32[128,896]{0,1:T(8,128)}) %reduce-scatter.9.cloned.1.call-update) | async-done | bytes 458768 | tf_op jit(solution)/shard_map/reduce_scatter | solution.py:32
  116.6 31.8 %reduce-scatter.5.cloned.1.call-done = f32[128,1792]{0,1:T(8,128)} async-done(((f32[256,1792]{0,1:T(8,128)}), f32[128,1792]{0,1:T(8,128)}) %reduce-scatter.5.cloned.1.call-update) | async-done | bytes 917520 | tf_op jit(solution)/shard_map/reduce_scatter | solution.py:32
  148.3 1.6 multiply_convert_fusion.1
  149.9 13.1 %all_gather.15 = bf16[256,1792]{0,1:T(8,128)(2,1)S(1)} all-gather(bf16[128,1792]{0,1:T(8,128)(2,1)S(1)} %pad_maximum_fusion.7), channel_id=1, replica_groups=mesh['row'=2,'col'=4,'depth'=4] {'row'}, dimensions={0}, use_global_device_ids=true | all-gather | bytes 1376256 | tf_op jit(solution)/shard_map/all_gather | solution.py:38
  163.1 8.3 %fusion.4 = bf16[256,4096]{1,0:T(8,128)(2,1)} fusion(bf16[256,1792]{0,1:T(8,128)(2,1)S(1)} %all_gather.15, bf16[4096,896]{0,1:T(8,128)(2,1)} %get-tuple-element.15, bf16[4096,896]{0,1:T(8,128)(2,1)} %get-tuple-element.16), kind=kOutput, calls=%fused_computation.12 | convolution fusion | flops 3788505088 | bytes 17694720 | tf_op jit(solution)/shard_map/dot_general | solution.py:95
  171.4 0.0 reduce-scatter.11.cloned.1.call-update
  171.4 0.0 reduce-scatter.7.cloned.1.call-start
  171.5 7.1 %all_gather.13 = bf16[256,896]{0,1:T(8,128)(2,1)S(1)} all-gather(bf16[128,896]{0,1:T(8,128)(2,1)S(1)} %get-tuple-element.14), channel_id=1, replica_groups=mesh['row'=2,'col'=4,'depth'=4] {'row'}, dimensions={0}, use_global_device_ids=true | all-gather | bytes 688128 | tf_op jit(solution)/shard_map/all_gather | solution.py:38
  178.6 0.0 copy-start.1
  178.6 9.1 %convolution_convert_fusion = bf16[256,4096]{1,0:T(8,128)(2,1)} fusion(bf16[256,896]{0,1:T(8,128)(2,1)S(1)} %all_gather.13, bf16[896,4096]{1,0:T(8,128)(2,1)} %param.11, pred[112,8,32,128]{3,2,1,0:T(32,128)(4,1)} %bitcast.48), kind=kOutput, calls=%fused_computation.13 | convolution fusion | flops 1883766784 | bytes 13565952 | tf_op jit(solution)/shard_map/dot_general | solution.py:80
  187.7 0.0 reduce-scatter.7.cloned.1.call-update
  187.8 0.0 copy-done.1
  187.8 7.2 %convolution_bitcast_fusion = bf16[4096,1792]{0,1:T(8,128)(2,1)} fusion(bf16[256,1792]{0,1:T(8,128)(2,1)S(1)} %all_gather.15, bf16[256,4096]{1,0:T(8,128)(2,1)S(1)} %copy-done.1), kind=kOutput, calls=%fused_computation.4 | convolution fusion | flops 3758096384 | bytes 17694720 | tf_op jit(solution)/shard_map/dot_general | solution.py:87
  195.0 12.1 %fusion.1 = (bf16[4096,896]{0,1:T(8,128)(2,1)}, bf16[4096,896]{0,1:T(8,128)(2,1)}) fusion(bf16[4096,1792]{0,1:T(8,128)(2,1)} %convolution_bitcast_fusion, pred[4096,7]{0,1:T(8,128)(4,1)S(1)} %bitcast.52, pred[4096,7]{0,1:T(8,128)(4,1)S(1)} %bitcast.54), kind=kLoop, calls=%fused_computation.6 | loop fusion | flops 7340032 | bytes 29417472 | tf_op jit(solution)/shard_map/convert_element_type | solution.py:92
  207.1 10.9 %copy.15 = bf16[4096,896]{1,0:T(8,128)(2,1)} copy(bf16[4096,896]{0,1:T(8,128)(2,1)} %get-tuple-element.11) | data formatting | bytes 14680064
  217.9 0.0 copy-start.3
  217.9 11.1 %copy.16 = bf16[4096,896]{1,0:T(8,128)(2,1)} copy(bf16[4096,896]{0,1:T(8,128)(2,1)} %get-tuple-element.10) | data formatting | bytes 14680064
  229.0 0.0 copy-done.3
  229.0 7.8 %select_convert_fusion = bf16[896,4096]{1,0:T(8,128)(2,1)} fusion(pred[112,8,32,128]{3,2,1,0:T(32,128)(4,1)} %bitcast.49, bf16[256,896]{0,1:T(8,128)(2,1)S(1)} %all_gather.13, bf16[256,4096]{1,0:T(8,128)(2,1)S(1)} %copy-done.3), kind=kOutput, calls=%fused_computation.8 | convolution fusion | flops 1886388224 | bytes 13565952 | tf_op jit(solution)/shard_map/dot_general | solution.py:83
  236.8 0.0 reduce-scatter.11.cloned.1.call-done
  236.8 61.6 %reduce-scatter.7.cloned.1.call-done = bf16[16,4096]{1,0:T(8,128)(2,1)} async-done(((bf16[256,4096]{1,0:T(8,128)(2,1)}), bf16[16,4096]{1,0:T(8,128)(2,1)}) %reduce-scatter.7.cloned.1.call-update) | async-done | bytes 131088 | tf_op jit(solution)/shard_map/reduce_scatter | solution.py:42
  (5 shorter events, 0.1 us)
Async XLA Ops:
  7.2 47.1 %all-gather.5.cloned.1.call-start = ((), (), s32[]{:S(2)}) async-start(), calls=%async_computation.7 | async-start | bytes 2228224 | tf_op jit(solution)/shard_map/all_gather | solution.py:62
  7.9 93.6 %all-gather.3.cloned.1.call-start = ((), (), s32[]{:S(2)}) async-start(), calls=%async_computation.4 | async-start | bytes 2228224 | tf_op jit(solution)/shard_map/all_gather | solution.py:61
  8.6 107.9 %reduce-scatter.9.cloned.1.call-start = ((), (), s32[]{:S(2)}) async-start(), calls=%async_computation.8 | async-start | bytes 1376256 | tf_op jit(solution)/shard_map/reduce_scatter | solution.py:32
  59.5 1.8 copy-start
  61.3 8.0 %copy-start.2 = (s32[32,7]{0,1:T(8,128)S(1)}, s32[32,7]{0,1:T(8,128)}, u32[]{:S(2)}) copy-start(s32[32,7]{0,1:T(8,128)} %param.12) | copy-start | bytes 2692
  69.2 79.1 %reduce-scatter.5.cloned.1.call-start = ((), (), s32[]{:S(2)}) async-start(), calls=%async_computation.5 | async-start | bytes 2752512 | tf_op jit(solution)/shard_map/reduce_scatter | solution.py:32
  113.0 123.9 %reduce-scatter.11.cloned.1.call-start = ((), (), s32[]{:S(2)}) async-start(), calls=%async_computation.9 | async-start | bytes 2228224 | tf_op jit(solution)/shard_map/reduce_scatter | solution.py:42
  171.4 127.0 %reduce-scatter.7.cloned.1.call-start = ((), (), s32[]{:S(2)}) async-start(), calls=%async_computation.6 | async-start | bytes 2228224 | tf_op jit(solution)/shard_map/reduce_scatter | solution.py:42
  178.6 9.2 %copy-start.1 = (bf16[256,4096]{1,0:T(8,128)(2,1)S(1)}, bf16[256,4096]{1,0:T(8,128)(2,1)}, u32[]{:S(2)}) copy-start(bf16[256,4096]{1,0:T(8,128)(2,1)} %all-gather.3.cloned.1.call-done) | copy-start | bytes 6291460
  217.9 11.1 %copy-start.3 = (bf16[256,4096]{1,0:T(8,128)(2,1)S(1)}, bf16[256,4096]{1,0:T(8,128)(2,1)}, u32[]{:S(2)}) copy-start(bf16[256,4096]{1,0:T(8,128)(2,1)} %all-gather.5.cloned.1.call-done) | copy-start | bytes 6291460
Sparse Core Ops, SparseCore 0:
  10.2 44.0 all-gather.4
  56.5 40.1 all-gather.2
  98.9 17.6 reduce-scatter.8
  119.3 28.9 reduce-scatter.4
  171.6 61.5 reduce-scatter.10
  237.8 60.6 reduce-scatter.6
where the time goes:
time: 306 us; the launch traced here: 305 us
  waiting for transfers between devices  142 us (46%)
  matrix products  51.8 us (17%)
  local copies, waits for them, and re-layouts  50.8 us (17%)
  other arithmetic  25.6 us (8%)
  blocking collectives  20.2 us (7%)
  between operations  14.2 us (5%)
    reduce_scatter x2, waiting for transfers between devices, group_sums(): lax.psum_scatter(term(jnp.int32(0), rows * lax.axis_size(('col', 'depth')...  61.6 us
    unnamed x16, local copies, waits for them, and re-layouts  45.6 us
    all_gather x1, waiting for transfers between devices, local(): lax.all_gather(grad_out, ('col', 'depth'), axis=0, tiled=True)  44.1 us
    reduce_scatter x2, waiting for transfers between devices, row_sums(): lax.psum_scatter(term(jnp.int32(0), lax.axis_size('row') * rows), 'row',...  35.3 us
    all_gather x2, blocking collectives, row_gather(): return lax.all_gather(block, 'row', axis=0, tiled=True)  20.2 us
    convert_element_type x1, other arithmetic, local(): jnp.where(keep_up, grad_both[:, width:], jnp.float32(0.0))  12.1 us
    dot_general x1, matrix products, hidden_term(): return jnp.dot(x_all, w_both, preferred_element_type=jnp.float32)  11.4 us
    select_n x1, other arithmetic, local(): jnp.where(keep_up, up_weight, zero_value)  10.5 us
  transfers between devices with their start and end apart: 6, of which 4 were waited for; matrix products, arithmetic and copies ran while one was open for 38% of the time, Pallas kernels for 0%

commit v1 on v0

v1 whole, which is shorter than its diff:
```python
import functools

import jax
import jax.numpy as jnp
from jax import lax
from jax.experimental import pallas as pl
from jax.experimental.pallas import tpu as pltpu
from jax.sharding import PartitionSpec as P

BLK = 128
PAIR = 2 * BLK
NCH = 4
F32 = jnp.float32
BF16 = jnp.bfloat16
MESH = pl.DeviceIdType.MESH
NT = (((1,), (1,)), ((), ()))
TN = (((0,), (0,)), ((), ()))


def masked(block, row):
    rows, lanes = block.shape
    keep = jnp.broadcast_to(row, (16, lanes)).astype(BF16)
    return (block.reshape(rows // 16, 16, lanes) * keep[None]).reshape(rows, lanes)


def fused(
    R, C,
    x_hbm, g_hbm, wg_hbm, wu_hbm, wd_hbm, kcat, kd,
    mixed, gtok, x_out, g_out, act_out, gc_out,
    x_all, g_all, wcat, wd, act, gc, hf, hb, hr, gf, gb, gr, part, r1, s1, r2, zb, r3,
    a_ss, a_rs, w_sem, h_ss, h_rs, act_ss, act_rs, ga_ss, ga_rs, gc_ss, gc_rs, q_ss, q_rs, o_sem,
):
    r, c, d = lax.axis_index("row"), lax.axis_index("col"), lax.axis_index("depth")
    rows, dl = x_hbm.shape
    tokens = x_all.shape[0]
    nj = wd.shape[0] // BLK
    ni = dl // BLK
    half = tokens // R
    ch = dl // NCH
    d1 = d + 1 - 2 * lax.rem(d, 2)
    d2 = lax.rem(d + 2, 4)
    d3 = lax.rem(d1 + 2, 4)
    own = pl.ds(pl.multiple_of(r * half, half), half)

    def remote(src, dst, ss, rs, dev):
        return pltpu.make_async_remote_copy(
            src_ref=src, dst_ref=dst, send_sem=ss, recv_sem=rs, device_id=dev, device_id_type=MESH
        )

    def col_at(k):
        return lax.rem(c + k, C)

    def row_at(k):
        return lax.rem(r + k, R)

    barrier = pltpu.get_barrier_semaphore()
    peers = [{"col": col_at(k)} for k in range(1, C)]
    peers += [{"row": row_at(k)} for k in range(1, R)]
    peers += [{"depth": d1}, {"depth": d2}]
    for dev in peers:
        pl.semaphore_signal(barrier, inc=1, device_id=dev, device_id_type=MESH)
    pl.semaphore_wait(barrier, len(peers))

    srcs, alls = (x_hbm, g_hbm), (x_all, g_all)

    def blk(cc, dd):
        return pl.ds(pl.multiple_of((cc * 4 + dd) * rows, rows), rows)

    def gather(a, slot, k):
        if slot == 0:
            dev, at = {"col": col_at(k)}, blk(c, d)
        elif slot == 1:
            dev, at = {"depth": d2}, blk(col_at(C - k), d)
        elif slot == 2:
            dev, at = {"depth": d1}, blk(col_at(C - k), d)
        else:
            dev, at = {"depth": d1}, blk(col_at(C - k), d2)
        src = srcs[a] if slot == 0 or (k == 0 and slot < 3) else alls[a].at[at]
        return remote(src, alls[a].at[at], a_ss.at[a, slot, k], a_rs.at[a, slot, k], dev)

    def arrived(a, slot, k):
        dd = (d, d2, d1, d3)[slot]
        at = blk(col_at(C - k), dd)
        remote(
            alls[a].at[at], alls[a].at[at], a_ss.at[a, slot, k], a_rs.at[a, slot, k], {"depth": d1}
        ).wait_recv()

    def local_own(a):
        return pltpu.make_async_copy(srcs[a], alls[a].at[blk(c, d)], o_sem.at[a])

    def gather_first(a):
        for k in range(C - 1, 0, -1):
            gather(a, 0, k).start()
        gather(a, 1, 0).start()
        gather(a, 2, 0).start()
        local_own(a).start()

    def gather_second(a):
        for k in range(1, C):
            arrived(a, 0, k)
            gather(a, 1, k).start()
            gather(a, 2, k).start()

    def gather_third(a):
        for k in range(C):
            arrived(a, 1, k)
            gather(a, 3, k).start()

    def gather_last(a):
        local_own(a).wait()
        for k in range(C):
            arrived(a, 2, k)
        for k in range(C):
            arrived(a, 3, k)

    def lanes(j, width):
        return pl.ds(pl.multiple_of(j * width, width), width)

    def w_copies(j):
        left = pl.ds(pl.multiple_of(j * PAIR, BLK), BLK)
        right = pl.ds(pl.multiple_of(j * PAIR + BLK, BLK), BLK)
        return (
            pltpu.make_async_copy(wg_hbm.at[:, lanes(j, BLK)], wcat.at[:, left], w_sem.at[0, j]),
            pltpu.make_async_copy(wu_hbm.at[:, lanes(j, BLK)], wcat.at[:, right], w_sem.at[1, j]),
        )

    def d_copy(j):
        return pltpu.make_async_copy(
            wd_hbm.at[lanes(j, BLK), :], wd.at[lanes(j, BLK), :], w_sem.at[2, j]
        )

    gather_first(0)
    for j in range(nj):
        for copy in w_copies(j):
            copy.start()
    for j in range(nj):
        d_copy(j).start()

    def mask_cat(j, carry):
        for copy in w_copies(j):
            copy.wait()
        cols = lanes(j, PAIR)

        def one(i, inner):
            at = lanes(i, BLK)
            wcat[at, cols] = masked(wcat[at, cols], kcat[pl.ds(i, 1), cols])
            return inner

        return lax.fori_loop(0, ni, one, carry)

    def mask_down(j, carry):
        d_copy(j).wait()

        def one(i, inner):
            at = lanes(i, dl // NCH)
            wd[lanes(j, BLK), at] = masked(wd[lanes(j, BLK), at], kd[pl.ds(j, 1), at])
            return inner

        return lax.fori_loop(0, NCH, one, carry)

    gather_second(0)
    gather_first(1)
    lax.fori_loop(0, nj, mask_cat, 0)
    gather_third(0)
    lax.fori_loop(0, nj, mask_down, 0)
    gather_last(0)

    def h_send(j, k):
        at = pl.ds(pl.multiple_of(row_at(k) * half, half), half)
        return remote(
            hb.at[at, lanes(j, PAIR)], hr.at[k - 1, :, lanes(j, PAIR)],
            h_ss.at[k - 1, j], h_rs.at[k - 1, j], {"row": row_at(k)},
        )

    def hidden(j, carry):
        cols = lanes(j, PAIR)
        value = jnp.dot(x_all[...], wcat[:, cols], preferred_element_type=F32)
        hf[:, cols] = value
        hb[:, cols] = value.astype(BF16)
        for k in range(1, R):
            h_send(j, k).start()
        return carry

    lax.fori_loop(0, nj, hidden, 0)
    x_copy = pltpu.make_async_copy(x_all, x_out, o_sem.at[2])
    x_copy.start()
    gather_second(1)

    def act_send(j, k):
        at = act.at[own, lanes(j, BLK)]
        return remote(at, at, act_ss.at[k - 1, j], act_rs.at[k - 1, j], {"row": row_at(k)})

    def activate(j, carry):
        cols = lanes(j, PAIR)
        total = hf[own, cols]
        for k in range(1, R):
            h_send(j, k).wait_recv()
            total = total + hr[k - 1, :, cols].astype(F32)
        hf[own, cols] = total
        gate, up = total[:, :BLK], total[:, BLK:]
        act[own, lanes(j, BLK)] = (gate * jax.nn.sigmoid(gate) * up).astype(BF16)
        for k in range(1, R):
            act_send(j, k).start()
        return carry

    lax.fori_loop(0, nj, activate, 0)
    gather_third(1)
    gather_last(1)
    g_copy = pltpu.make_async_copy(g_all, g_out, o_sem.at[3])
    g_copy.start()

    def ga_send(j, k):
        at = pl.ds(pl.multiple_of(row_at(k) * half, half), half)
        return remote(
            gb.at[at, lanes(j, BLK)], gr.at[k - 1, :, lanes(j, BLK)],
            ga_ss.at[k - 1, j], ga_rs.at[k - 1, j], {"row": row_at(k)},
        )

    def back(j, carry):
        cols = lanes(j, BLK)
        value = lax.dot_general(g_all[...], wd[cols, :], NT, preferred_element_type=F32)
        gf[:, cols] = value
        gb[:, cols] = value.astype(BF16)
        for k in range(1, R):
            ga_send(j, k).start()
        return carry

    lax.fori_loop(0, nj, back, 0)

    def peer_rows(k):
        return pl.ds(pl.multiple_of(row_at(R - k) * half, half), half)

    def act_wait(j, carry):
        for k in range(1, R):
            at = act.at[peer_rows(k), lanes(j, BLK)]
            remote(at, at, act_ss.at[k - 1, j], act_rs.at[k - 1, j], {"row": row_at(k)}).wait_recv()
        return carry

    lax.fori_loop(0, nj, act_wait, 0)
    act_copy = pltpu.make_async_copy(act, act_out, o_sem.at[4])
    act_copy.start()

    outs = (mixed, gtok)

    def send1(a, q, h):
        cols = pl.ds(q * ch, ch)
        dst = (d1, d3)[h]
        return remote(
            part.at[a, dst, :, cols], r1.at[a, h, :, cols],
            q_ss.at[a, q, h], q_rs.at[a, q, h], {"depth": d1},
        )

    def send2(a, q):
        cols = pl.ds(q * ch, ch)
        return remote(
            s1.at[a, :, cols], r2.at[a, :, cols], q_ss.at[a, q, 2], q_rs.at[a, q, 2], {"depth": d2}
        )

    def send3(a, q, k):
        cols = pl.ds(q * ch, ch)
        at = pl.ds(pl.multiple_of(col_at(k) * rows, rows), rows)
        return remote(
            zb.at[a, at, cols], r3.at[a, k - 1, :, cols],
            q_ss.at[a, q, 2 + k], q_rs.at[a, q, 2 + k], {"col": col_at(k)},
        )

    def stage_a(a, q):
        def tile(n, carry):
            cols = pl.ds(pl.multiple_of(q * ch + n * PAIR, PAIR), PAIR)
            if a == 0:
                value = jnp.dot(act[...], wd[:, cols], preferred_element_type=F32)
            else:
                value = lax.dot_general(gc[...], wcat[cols, :], NT, preferred_element_type=F32)
            value = value.astype(BF16)
            for cc in range(C):
                for dd in range(4):
                    at = (cc * 4 + dd) * rows
                    part[a, dd, cc * rows : (cc + 1) * rows, cols] = value[at : at + rows]
            return carry

        lax.fori_loop(0, ch // PAIR, tile, 0)
        send1(a, q, 1).start()
        send1(a, q, 0).start()

    def stage_b(a, q):
        cols = pl.ds(q * ch, ch)
        send1(a, q, 1).wait_recv()
        s1[a, :, cols] = (part[a, d2, :, cols].astype(F32) + r1[a, 1, :, cols].astype(F32)).astype(BF16)
        send2(a, q).start()

    def stage_c(a, q):
        cols = pl.ds(q * ch, ch)
        send1(a, q, 0).wait_recv()
        send2(a, q).wait_recv()
        total = part[a, d, :, cols].astype(F32) + r1[a, 0, :, cols].astype(F32)
        zb[a, :, cols] = (total + r2[a, :, cols].astype(F32)).astype(BF16)
        for k in range(C - 1, 0, -1):
            send3(a, q, k).start()

    def stage_d(a, q):
        cols = pl.ds(q * ch, ch)
        at = pl.ds(pl.multiple_of(c * rows, rows), rows)
        total = zb[a, at, cols].astype(F32)
        for k in range(1, C):
            send3(a, q, k).wait_recv()
            total = total + r3[a, k - 1, :, cols].astype(F32)
        outs[a][:, cols] = total.astype(BF16)

    for q in range(NCH):
        stage_a(0, q)
        if q > 0:
            stage_b(0, q - 1)
    stage_b(0, NCH - 1)

    def gc_send(j, k):
        at = gc.at[own, lanes(j, PAIR)]
        return remote(at, at, gc_ss.at[k - 1, j], gc_rs.at[k - 1, j], {"row": row_at(k)})

    def swiglu_back(j, carry):
        cols = lanes(j, BLK)
        grad = gf[own, cols]
        for k in range(1, R):
            ga_send(j, k).wait_recv()
            grad = grad + gr[k - 1, :, cols].astype(F32)
        both = hf[own, lanes(j, PAIR)]
        gate, up = both[:, :BLK], both[:, BLK:]
        sig = jax.nn.sigmoid(gate)
        gg = (grad * up * sig * (1.0 + gate * (1.0 - sig))).astype(BF16)
        gu = (grad * gate * sig).astype(BF16)
        gc[own, lanes(j, PAIR)] = jnp.concatenate([gg, gu], axis=1)
        for k in range(1, R):
            gc_send(j, k).start()
        return carry

    lax.fori_loop(0, nj, swiglu_back, 0)
    for q in range(NCH):
        stage_c(0, q)

    def gc_wait(j, carry):
        for k in range(1, R):
            at = gc.at[peer_rows(k), lanes(j, PAIR)]
            remote(at, at, gc_ss.at[k - 1, j], gc_rs.at[k - 1, j], {"row": row_at(k)}).wait_recv()
        return carry

    lax.fori_loop(0, nj, gc_wait, 0)
    gc_copy = pltpu.make_async_copy(gc, gc_out, o_sem.at[5])
    gc_copy.start()
    for q in range(NCH):
        stage_a(1, q)
        if q > 0:
            stage_b(1, q - 1)
        if q > 1:
            stage_c(1, q - 2)
    stage_b(1, NCH - 1)
    stage_c(1, NCH - 2)
    for q in range(NCH):
        stage_d(0, q)
    stage_c(1, NCH - 1)
    for q in range(NCH):
        stage_d(1, q)

    for a in range(2):
        for k in range(1, C):
            gather(a, 0, k).wait_send()
        for slot in range(1, 4):
            for k in range(C):
                gather(a, slot, k).wait_send()
        for q in range(NCH):
            send1(a, q, 0).wait_send()
            send1(a, q, 1).wait_send()
            send2(a, q).wait_send()
            for k in range(1, C):
                send3(a, q, k).wait_send()

    def drain(j, carry):
        for k in range(1, R):
            h_send(j, k).wait_send()
            act_send(j, k).wait_send()
            ga_send(j, k).wait_send()
            gc_send(j, k).wait_send()
        return carry

    lax.fori_loop(0, nj, drain, 0)
    x_copy.wait()
    g_copy.wait()
    act_copy.wait()
    gc_copy.wait()


def weight_grads(x_ref, g_ref, act_ref, gc_ref, kcat, kd, dg_ref, du_ref, dd_ref):
    width = x_ref.shape[1]
    nj = act_ref.shape[1] // BLK
    for j in range(nj):
        cols = slice(j * PAIR, (j + 1) * PAIR)
        value = lax.dot_general(x_ref[...], gc_ref[:, cols], TN, preferred_element_type=F32)
        value = value.astype(BF16)
        out = slice(j * BLK, (j + 1) * BLK)
        for i in range(width // BLK):
            at = slice(i * BLK, (i + 1) * BLK)
            block = masked(value[at], kcat[0, i : i + 1, cols])
            dg_ref[at, out] = block[:, :BLK]
            du_ref[at, out] = block[:, BLK:]
        down = lax.dot_general(act_ref[:, out], g_ref[...], TN, preferred_element_type=F32)
        dd_ref[out, :] = masked(down.astype(BF16), kd[j : j + 1, :])


def local(R, C, tokens, gate_weight, up_weight, down_weight, gate_mask, up_mask, down_mask, grad_out):
    rows, dl = tokens.shape
    hid = gate_weight.shape[1]
    total = rows * C * 4
    nj, ni = hid // BLK, dl // BLK
    half = total // R
    kcat = jnp.stack([gate_mask, up_mask], axis=2).reshape(ni, 2 * nj)
    kcat = jnp.repeat(kcat.astype(F32), BLK, axis=1)
    kd = jnp.repeat(down_mask.astype(F32), BLK, axis=1)
    any_spec = pl.BlockSpec(memory_space=pl.ANY)
    vmem = pl.BlockSpec(memory_space=pltpu.VMEM)
    part = (rows * C, dl)
    dma = pltpu.SemaphoreType.DMA
    S = jax.ShapeDtypeStruct
    mixed, gtok, x_all, g_all, act, gc = pl.pallas_call(
        functools.partial(fused, R, C),
        out_shape=(
            S((rows, dl), BF16), S((rows, dl), BF16), S((total, dl), BF16), S((total, dl), BF16),
            S((total, hid), BF16), S((total, 2 * hid), BF16),
        ),
        in_specs=[any_spec] * 5 + [vmem] * 2,
        out_specs=(vmem, vmem, any_spec, any_spec, any_spec, any_spec),
        scratch_shapes=[
            pltpu.VMEM((total, dl), BF16),
            pltpu.VMEM((total, dl), BF16),
            pltpu.VMEM((dl, 2 * hid), BF16),
            pltpu.VMEM((hid, dl), BF16),
            pltpu.VMEM((total, hid), BF16),
            pltpu.VMEM((total, 2 * hid), BF16),
            pltpu.VMEM((total, 2 * hid), F32),
            pltpu.VMEM((total, 2 * hid), BF16),
            pltpu.VMEM((R - 1, half, 2 * hid), BF16),
            pltpu.VMEM((total, hid), F32),
            pltpu.VMEM((total, hid), BF16),
            pltpu.VMEM((R - 1, half, hid), BF16),
            pltpu.VMEM((2, 4) + part, BF16),
            pltpu.VMEM((2, 2) + part, BF16),
            pltpu.VMEM((2,) + part, BF16),
            pltpu.VMEM((2,) + part, BF16),
            pltpu.VMEM((2,) + part, BF16),
            pltpu.VMEM((2, C - 1, rows, dl), BF16),
            dma((2, 4, C)), dma((2, 4, C)), dma((3, nj)),
            dma((R - 1, nj)), dma((R - 1, nj)), dma((R - 1, nj)), dma((R - 1, nj)),
            dma((R - 1, nj)), dma((R - 1, nj)), dma((R - 1, nj)), dma((R - 1, nj)),
            dma((2, NCH, 2 + C)), dma((2, NCH, 2 + C)), dma((6,)),
        ],
        compiler_params=pltpu.CompilerParams(
            collective_id=0, has_side_effects=True, vmem_limit_bytes=60 * 2**20
        ),
        name="layer",
    )(tokens, grad_out, gate_weight, up_weight, down_weight, kcat, kd)

    width = 512
    whole = lambda i: (0, 0)
    dg, du, dd = pl.pallas_call(
        weight_grads,
        grid=(dl // width,),
        out_shape=(S((dl, hid), BF16), S((dl, hid), BF16), S((hid, dl), BF16)),
        in_specs=[
            pl.BlockSpec((total, width), lambda i: (0, i)),
            pl.BlockSpec((total, width), lambda i: (0, i)),
            pl.BlockSpec((total, hid), whole),
            pl.BlockSpec((total, 2 * hid), whole),
            pl.BlockSpec((1, width // BLK, 2 * hid), lambda i: (i, 0, 0)),
            pl.BlockSpec((nj, width), lambda i: (0, i)),
        ],
        out_specs=(
            pl.BlockSpec((width, hid), lambda i: (i, 0)),
            pl.BlockSpec((width, hid), lambda i: (i, 0)),
            pl.BlockSpec((hid, width), lambda i: (0, i)),
        ),
        compiler_params=pltpu.CompilerParams(vmem_limit_bytes=60 * 2**20),
        name="weight_grads",
    )(x_all, g_all, act, gc, kcat.reshape(dl // width, width // BLK, 2 * hid), kd)
    return (mixed, gtok, dg, du, dd)


def solution(mesh):
    return jax.shard_map(
        functools.partial(local, mesh.shape["row"], mesh.shape["col"]),
        mesh=mesh,
        in_specs=(
            P(("col", "depth"), "row"),
            P("row", ("col", "depth")),
            P("row", ("col", "depth")),
            P(("col", "depth"), "row"),
            P("row", ("col", "depth")),
            P("row", ("col", "depth")),
            P(("col", "depth"), "row"),
            P(("col", "depth"), "row"),
        ),
        out_specs=(
            P(("col", "depth"), "row"),
            P(("col", "depth"), "row"),
            P("row", ("col", "depth")),
            P("row", ("col", "depth")),
            P(("col", "depth"), "row"),
        ),
        check_vma=False,
    )
```

time: 306 us -> 116 us (0.38)
  waiting for transfers between devices: 142 us -> 0 us
  Pallas kernels: 0 us -> 108 us
  matrix products: 51.8 us -> 0 us
  local copies, waits for them, and re-layouts: 50.8 us -> 5.73 us
  other arithmetic: 25.6 us -> 1.4 us
  blocking collectives: 20.2 us -> 0 us
  between operations: 14.2 us -> 0.66 us
    pallas_call x0 -> x2, Pallas kernels: none -> 108 us  [the longest x1 95.1 us: local(): pl.pallas_call(functools.partial(fused, R, C), out_shape=(S((rows, dl), B...]
    reduce_scatter x4 -> x0, waiting for transfers between devices: 96.9 us -> none  [the longest x2 61.6 us: group_sums(): lax.psum_scatter(term(jnp.int32(0), rows * lax.axis_size(('col', 'depth')...]
    dot_general x6 -> x0, matrix products: 51.8 us -> none  [the longest x1 11.4 us: hidden_term(): return jnp.dot(x_all, w_both, preferred_element_type=jnp.float32)]
    all_gather x2 -> x0, waiting for transfers between devices: 44.1 us -> none  [the longest x1 44.1 us: local(): lax.all_gather(grad_out, ('col', 'depth'), axis=0, tiled=True)]
    unnamed x16 -> x5, local copies, waits for them, and re-layouts: 45.6 us -> 4.72 us
    all_gather x2 -> x0, blocking collectives: 20.2 us -> none  [row_gather(): return lax.all_gather(block, 'row', axis=0, tiled=True)]
    convert_element_type x1 -> x2, other arithmetic: 12.1 us -> 1.4 us  [the longest x1 0.71 us: local(): kcat = jnp.repeat(kcat.astype(F32), BLK, axis=1)]
    select_n x1 -> x0, other arithmetic: 10.5 us -> none  [local(): jnp.where(keep_up, up_weight, zero_value)]
  transfers between devices with their start and end apart: 6 -> 0, of which waited for: 4 -> 0; matrix products, arithmetic and copies ran while one was open for 38% -> 0% of each run, Pallas kernels for 0% -> 0%
where the time goes in v1:
time: 116 us
  Pallas kernels  108 us (93%)
  local copies, waits for them, and re-layouts  5.73 us (5%)
  other arithmetic  1.4 us (1%)
    pallas_call x1, Pallas kernels, local(): pl.pallas_call(functools.partial(fused, R, C), out_shape=(S((rows, dl), B...  95.1 us
    pallas_call x1, Pallas kernels, local(): pl.pallas_call(weight_grads, grid=(dl // width,), out_shape=(S((dl, hid),...  12.7 us
    unnamed x5, local copies, waits for them, and re-layouts  4.72 us

profile of v1, /device:TPU:0, one launch (start us, length us, event | category | flops | bytes accessed | tf_op | source)
XLA Modules:
  0.0 115.6 jit_solution(7026407575976401501)
XLA Ops:
  0.6 0.7 convert_element_type.11
  1.3 0.7 add_convert_fusion
  2.0 0.1 copy.14
  2.1 0.1 broadcast_bitcast_fusion
  2.2 0.7 copy.20
  3.0 0.1 broadcast_in_dim.6
  3.1 0.8 copy.19
  3.9 0.8 reshape_reshape.3.kcat
  4.6 95.1 %layer.1 = (bf16[16,4096]{1,0:T(8,128)(2,1)}, bf16[16,4096]{1,0:T(8,128)(2,1)}, bf16[256,4096]{1,0:T(8,128)(2,1)}, bf16[256,4096]{1,0:T(8,128)(2,1)}, bf16[256,8...) custom-call(bf16[16,4096]{1,0:T(8,128)(2,1)} %x_hbm.1, bf16[16,4096]{1,0:T(8,128)(2,1)} %g_hbm.1, bf16[4096,896]{1,0:T(8,128)(2,1)} %wg_hbm.1, ...), custom_call_target="tpu_custom_call" | custom-call | tf_op jit(solution)/shard_map/layer/pallas_call | solution.py:421
  99.8 12.7 %weight_grads.1 = (bf16[4096,896]{1,0:T(8,128)(2,1)}, bf16[4096,896]{1,0:T(8,128)(2,1)}, bf16[896,4096]{1,0:T(8,128)(2,1)}) custom-call(bf16[256,4096]{1,0:T(8,128)(2,1)} %get-tuple-element.16.x_ref, bf16[256,4096]{1,0:T(8,128)(2,1)} %get-tuple-element.17.g_ref, bf16[256,896]{1,0:T(8,128)(2,1)} %get-tuple-element.18.act_ref, ...), custom_call_target="tpu_custom_call" | custom-call | tf_op jit(solution)/shard_map/weight_grads/pallas_call | solution.py:461
  112.4 1.6 %copy.23 = bf16[16,4096]{1,0:T(8,128)(2,1)} copy(bf16[16,4096]{1,0:T(8,128)(2,1)} %get-tuple-element.28) | data formatting | bytes 262144
  114.0 1.6 %copy.24 = bf16[16,4096]{1,0:T(8,128)(2,1)} copy(bf16[16,4096]{1,0:T(8,128)(2,1)} %get-tuple-element.29) | data formatting | bytes 262144
  (2 shorter events, 0.0 us)

commit v2 on v1

--- a/solution.py
+++ b/solution.py
@@ -17,15 +17,16 @@
 TN = (((0,), (0,)), ((), ()))
 
 
-def masked(block, row):
+def masked(block, *keeps):
     rows, lanes = block.shape
-    keep = jnp.broadcast_to(row, (16, lanes)).astype(BF16)
+    keep = [jnp.full((16, BLK), k, jnp.int32).astype(F32).astype(BF16) for k in keeps]
+    keep = jnp.concatenate(keep, axis=1)
     return (block.reshape(rows // 16, 16, lanes) * keep[None]).reshape(rows, lanes)
 
 
 def fused(
     R, C,
-    x_hbm, g_hbm, wg_hbm, wu_hbm, wd_hbm, kcat, kd,
+    x_hbm, g_hbm, wg_hbm, wu_hbm, wd_hbm, kg, ku, kd,
     mixed, gtok, x_out, g_out, act_out, gc_out,
     x_all, g_all, wcat, wd, act, gc, hf, hb, hr, gf, gb, gr, part, r1, s1, r2, zb, r3,
     a_ss, a_rs, w_sem, h_ss, h_rs, act_ss, act_rs, ga_ss, ga_rs, gc_ss, gc_rs, q_ss, q_rs, o_sem,
@@ -66,45 +67,58 @@
     def blk(cc, dd):
         return pl.ds(pl.multiple_of((cc * 4 + dd) * rows, rows), rows)
 
-    def gather(a, slot, k):
-        if slot == 0:
-            dev, at = {"col": col_at(k)}, blk(c, d)
-        elif slot == 1:
+    def hop(a, slot, k):
+        if slot == 1:
             dev, at = {"depth": d2}, blk(col_at(C - k), d)
         elif slot == 2:
             dev, at = {"depth": d1}, blk(col_at(C - k), d)
         else:
             dev, at = {"depth": d1}, blk(col_at(C - k), d2)
-        src = srcs[a] if slot == 0 or (k == 0 and slot < 3) else alls[a].at[at]
+        src = srcs[a] if k == 0 and slot < 3 else alls[a].at[at]
         return remote(src, alls[a].at[at], a_ss.at[a, slot, k], a_rs.at[a, slot, k], dev)
 
     def arrived(a, slot, k):
-        dd = (d, d2, d1, d3)[slot]
+        dd = (d, d2, d1, d3, d2)[slot]
         at = blk(col_at(C - k), dd)
         remote(
             alls[a].at[at], alls[a].at[at], a_ss.at[a, slot, k], a_rs.at[a, slot, k], {"depth": d1}
         ).wait_recv()
 
+    def chain(a, slot, way, k):
+        index = k if way > 0 else C - k
+        back = k - 1 if way > 0 else C - k + 1
+        at = blk(col_at(C - back), d if slot == 0 else d2)
+        src = srcs[a] if slot == 0 and k == 1 else alls[a].at[at]
+        dev = {"col": col_at(1 if way > 0 else C - 1)}
+        return remote(
+            src, alls[a].at[at], a_ss.at[a, slot, index], a_rs.at[a, slot, index], dev
+        )
+
+    def chain_sends(way, k):
+        if way > 0:
+            return jnp.logical_and(c >= k - 1, c < C - 1)
+        return jnp.logical_and(c + k - 1 <= C - 1, c > 0)
+
+    def chain_start(a, slot, k, way):
+        @pl.when(chain_sends(way, k))
+        def _():
+            chain(a, slot, way, k).start()
+
+    def chain_step(a, slot, k, onward):
+        for way in (1, -1):
+            here = c >= k if way > 0 else c + k <= C - 1
+            index = k if way > 0 else C - k
+
+            @pl.when(here)
+            def _():
+                arrived(a, slot, index)
+                if k < C - 1:
+                    chain_start(a, slot, k + 1, way)
+                for other in onward:
+                    hop(a, other, index).start()
+
     def local_own(a):
         return pltpu.make_async_copy(srcs[a], alls[a].at[blk(c, d)], o_sem.at[a])
-
-    def gather_first(a):
-        for k in range(C - 1, 0, -1):
-            gather(a, 0, k).start()
-        gather(a, 1, 0).start()
-        gather(a, 2, 0).start()
-        local_own(a).start()
-
-    def gather_second(a):
-        for k in range(1, C):
-            arrived(a, 0, k)
-            gather(a, 1, k).start()
-            gather(a, 2, k).start()
-
-    def gather_third(a):
-        for k in range(C):
-            arrived(a, 1, k)
-            gather(a, 3, k).start()
 
     def gather_last(a):
         local_own(a).wait()
@@ -129,7 +143,12 @@
             wd_hbm.at[lanes(j, BLK), :], wd.at[lanes(j, BLK), :], w_sem.at[2, j]
         )
 
-    gather_first(0)
+    for way in (1, -1):
+        chain_start(0, 0, 1, way)
+    hop(0, 1, 0).start()
+    hop(1, 1, 0).start()
+    hop(0, 2, 0).start()
+    local_own(0).start()
     for j in range(nj):
         for copy in w_copies(j):
             copy.start()
@@ -143,7 +162,7 @@
 
         def one(i, inner):
             at = lanes(i, BLK)
-            wcat[at, cols] = masked(wcat[at, cols], kcat[pl.ds(i, 1), cols])
+            wcat[at, cols] = masked(wcat[at, cols], kg[j, i], ku[j, i])
             return inner
 
         return lax.fori_loop(0, ni, one, carry)
@@ -152,17 +171,32 @@
         d_copy(j).wait()
 
         def one(i, inner):
-            at = lanes(i, dl // NCH)
-            wd[lanes(j, BLK), at] = masked(wd[lanes(j, BLK), at], kd[pl.ds(j, 1), at])
+            at = lanes(i, PAIR)
+            wd[lanes(j, BLK), at] = masked(wd[lanes(j, BLK), at], kd[j, 2 * i], kd[j, 2 * i + 1])
             return inner
 
-        return lax.fori_loop(0, NCH, one, carry)
-
-    gather_second(0)
-    gather_first(1)
-    lax.fori_loop(0, nj, mask_cat, 0)
-    gather_third(0)
-    lax.fori_loop(0, nj, mask_down, 0)
+        return lax.fori_loop(0, ni // 2, one, carry)
+
+    cuts = [nj * n // 3 for n in range(4)]
+    chain_step(0, 0, 1, (1, 2))
+    for way in (1, -1):
+        chain_start(1, 0, 1, way)
+    hop(1, 2, 0).start()
+    local_own(1).start()
+    arrived(1, 1, 0)
+    for way in (1, -1):
+        chain_start(1, 4, 1, way)
+    hop(1, 3, 0).start()
+    lax.fori_loop(cuts[0], cuts[1], mask_cat, 0)
+    for k in range(2, C):
+        chain_step(0, 0, k, (1, 2))
+        chain_step(1, 0, k - 1, (2,))
+        chain_step(1, 4, k - 1, (3,))
+    lax.fori_loop(cuts[1], cuts[2], mask_cat, 0)
+    for k in range(C):
+        arrived(0, 1, k)
+        hop(0, 3, k).start()
+    lax.fori_loop(cuts[2], cuts[3], mask_cat, 0)
     gather_last(0)
 
     def h_send(j, k):
@@ -181,10 +215,13 @@
             h_send(j, k).start()
         return carry
 
-    lax.fori_loop(0, nj, hidden, 0)
+    lax.fori_loop(0, nj // 2, hidden, 0)
+    chain_step(1, 0, C - 1, (2,))
+    chain_step(1, 4, C - 1, (3,))
+    lax.fori_loop(nj // 2, nj, hidden, 0)
     x_copy = pltpu.make_async_copy(x_all, x_out, o_sem.at[2])
     x_copy.start()
-    gather_second(1)
+    lax.fori_loop(0, nj, mask_down, 0)
 
     def act_send(j, k):
         at = act.at[own, lanes(j, BLK)]
@@ -204,7 +241,6 @@
         return carry
 
     lax.fori_loop(0, nj, activate, 0)
-    gather_third(1)
     gather_last(1)
     g_copy = pltpu.make_async_copy(g_all, g_out, o_sem.at[3])
     g_copy.start()
@@ -360,11 +396,19 @@
         stage_d(1, q)
 
     for a in range(2):
-        for k in range(1, C):
-            gather(a, 0, k).wait_send()
-        for slot in range(1, 4):
-            for k in range(C):
-                gather(a, slot, k).wait_send()
+        for slot in (0, 4) if a == 1 else (0,):
+            for way in (1, -1):
+                for k in range(1, C):
+
+                    @pl.when(chain_sends(way, k))
+                    def _():
+                        chain(a, slot, way, k).wait_send()
+
+        for k in range(C):
+            if a == 0 or k == 0:
+                hop(a, 1, k).wait_send()
+            hop(a, 2, k).wait_send()
+            hop(a, 3, k).wait_send()
         for q in range(NCH):
             send1(a, q, 0).wait_send()
             send1(a, q, 1).wait_send()
@@ -387,32 +431,37 @@
     gc_copy.wait()
 
 
-def weight_grads(x_ref, g_ref, act_ref, gc_ref, kcat, kd, dg_ref, du_ref, dd_ref):
+def weight_grads(
+    x_ref, g_ref, act_ref, gc_ref, kg, ku, kd, mixed_in, gtok_in, dg_ref, du_ref, dd_ref, mixed, gtok
+):
     width = x_ref.shape[1]
+    first = pl.program_id(0) * (width // BLK)
     nj = act_ref.shape[1] // BLK
+    mixed[...] = mixed_in[...]
+    gtok[...] = gtok_in[...]
     for j in range(nj):
         cols = slice(j * PAIR, (j + 1) * PAIR)
         value = lax.dot_general(x_ref[...], gc_ref[:, cols], TN, preferred_element_type=F32)
         value = value.astype(BF16)
         out = slice(j * BLK, (j + 1) * BLK)
+        down = lax.dot_general(act_ref[:, out], g_ref[...], TN, preferred_element_type=F32)
+        down = down.astype(BF16)
         for i in range(width // BLK):
             at = slice(i * BLK, (i + 1) * BLK)
-            block = masked(value[at], kcat[0, i : i + 1, cols])
+            block = masked(value[at], kg[j, first + i], ku[j, first + i])
             dg_ref[at, out] = block[:, :BLK]
             du_ref[at, out] = block[:, BLK:]
-        down = lax.dot_general(act_ref[:, out], g_ref[...], TN, preferred_element_type=F32)
-        dd_ref[out, :] = masked(down.astype(BF16), kd[j : j + 1, :])
+            dd_ref[out, at] = masked(down[:, at], kd[j, first + i])
 
 
 def local(R, C, tokens, gate_weight, up_weight, down_weight, gate_mask, up_mask, down_mask, grad_out):
     rows, dl = tokens.shape
     hid = gate_weight.shape[1]
     total = rows * C * 4
-    nj, ni = hid // BLK, dl // BLK
+    nj = hid // BLK
     half = total // R
-    kcat = jnp.stack([gate_mask, up_mask], axis=2).reshape(ni, 2 * nj)
-    kcat = jnp.repeat(kcat.astype(F32), BLK, axis=1)
-    kd = jnp.repeat(down_mask.astype(F32), BLK, axis=1)
+    masks = (gate_mask.T, up_mask.T, down_mask)
+    smem = pl.BlockSpec(memory_space=pltpu.SMEM)
     any_spec = pl.BlockSpec(memory_space=pl.ANY)
     vmem = pl.BlockSpec(memory_space=pltpu.VMEM)
     part = (rows * C, dl)
@@ -424,7 +473,7 @@
             S((rows, dl), BF16), S((rows, dl), BF16), S((total, dl), BF16), S((total, dl), BF16),
             S((total, hid), BF16), S((total, 2 * hid), BF16),
         ),
-        in_specs=[any_spec] * 5 + [vmem] * 2,
+        in_specs=[any_spec] * 5 + [smem] * 3,
         out_specs=(vmem, vmem, any_spec, any_spec, any_spec, any_spec),
         scratch_shapes=[
             pltpu.VMEM((total, dl), BF16),
@@ -445,7 +494,7 @@
             pltpu.VMEM((2,) + part, BF16),
             pltpu.VMEM((2,) + part, BF16),
             pltpu.VMEM((2, C - 1, rows, dl), BF16),
-            dma((2, 4, C)), dma((2, 4, C)), dma((3, nj)),
+            dma((2, 5, C)), dma((2, 5, C)), dma((3, nj)),
             dma((R - 1, nj)), dma((R - 1, nj)), dma((R - 1, nj)), dma((R - 1, nj)),
             dma((R - 1, nj)), dma((R - 1, nj)), dma((R - 1, nj)), dma((R - 1, nj)),
             dma((2, NCH, 2 + C)), dma((2, NCH, 2 + C)), dma((6,)),
@@ -454,30 +503,38 @@
             collective_id=0, has_side_effects=True, vmem_limit_bytes=60 * 2**20
         ),
         name="layer",
-    )(tokens, grad_out, gate_weight, up_weight, down_weight, kcat, kd)
+    )(tokens, grad_out, gate_weight, up_weight, down_weight, *masks)
 
     width = 512
     whole = lambda i: (0, 0)
-    dg, du, dd = pl.pallas_call(
+    dg, du, dd, mixed, gtok = pl.pallas_call(
         weight_grads,
         grid=(dl // width,),
-        out_shape=(S((dl, hid), BF16), S((dl, hid), BF16), S((hid, dl), BF16)),
+        out_shape=(
+            S((dl, hid), BF16), S((dl, hid), BF16), S((hid, dl), BF16),
+            S((rows, dl), BF16), S((rows, dl), BF16),
+        ),
         in_specs=[
             pl.BlockSpec((total, width), lambda i: (0, i)),
             pl.BlockSpec((total, width), lambda i: (0, i)),
             pl.BlockSpec((total, hid), whole),
             pl.BlockSpec((total, 2 * hid), whole),
-            pl.BlockSpec((1, width // BLK, 2 * hid), lambda i: (i, 0, 0)),
-            pl.BlockSpec((nj, width), lambda i: (0, i)),
+            smem,
+            smem,
+            smem,
+            pl.BlockSpec((rows, width), lambda i: (0, i)),
+            pl.BlockSpec((rows, width), lambda i: (0, i)),
         ],
         out_specs=(
             pl.BlockSpec((width, hid), lambda i: (i, 0)),
             pl.BlockSpec((width, hid), lambda i: (i, 0)),
             pl.BlockSpec((hid, width), lambda i: (0, i)),
+            pl.BlockSpec((rows, width), lambda i: (0, i)),
+            pl.BlockSpec((rows, width), lambda i: (0, i)),
         ),
         compiler_params=pltpu.CompilerParams(vmem_limit_bytes=60 * 2**20),
         name="weight_grads",
-    )(x_all, g_all, act, gc, kcat.reshape(dl // width, width // BLK, 2 * hid), kd)
+    )(x_all, g_all, act, gc, *masks, mixed, gtok)
     return (mixed, gtok, dg, du, dd)
 
 

time: 116 us -> 107 us (0.922)
  local copies, waits for them, and re-layouts: 5.73 us -> 0 us
  Pallas kernels: 108 us -> 106 us
  other arithmetic: 1.4 us -> 0 us
    unnamed x5 -> x0, local copies, waits for them, and re-layouts: 4.72 us -> none
    pallas_call x1, Pallas kernels: 95.1 us -> 93.4 us  [local(): pl.pallas_call(functools.partial(fused, R, C), out_shape=(S((rows, dl), B...]
    convert_element_type x2 -> x0, other arithmetic: 1.4 us -> none  [the longest x1 0.71 us: local(): kcat = jnp.repeat(kcat.astype(F32), BLK, axis=1)]
where the time goes in v2:
time: 107 us
  Pallas kernels  106 us (99%)
    pallas_call x1, Pallas kernels, local(): pl.pallas_call(functools.partial(fused, R, C), out_shape=(S((rows, dl), B...  93.4 us
    pallas_call x1, Pallas kernels, local(): pl.pallas_call(weight_grads, grid=(dl // width,), out_shape=(S((dl, hid),...  12.7 us

profile of v2, /device:TPU:0, one launch (start us, length us, event | category | flops | bytes accessed | tf_op | source)
XLA Modules:
  0.0 106.8 jit_solution(12933992298688550811)
XLA Ops:
  0.6 93.4 %layer.1 = (bf16[16,4096]{1,0:T(8,128)(2,1)}, bf16[16,4096]{1,0:T(8,128)(2,1)}, bf16[256,4096]{1,0:T(8,128)(2,1)}, bf16[256,4096]{1,0:T(8,128)(2,1)}, bf16[256,8...) custom-call(bf16[16,4096]{1,0:T(8,128)(2,1)} %x_hbm.1, bf16[16,4096]{1,0:T(8,128)(2,1)} %g_hbm.1, bf16[4096,896]{1,0:T(8,128)(2,1)} %wg_hbm.1, ...), custom_call_target="tpu_custom_call" | custom-call | tf_op jit(solution)/shard_map/layer/pallas_call | solution.py:470
  94.0 12.7 %weight_grads.1 = (bf16[4096,896]{1,0:T(8,128)(2,1)}, bf16[4096,896]{1,0:T(8,128)(2,1)}, bf16[896,4096]{1,0:T(8,128)(2,1)}, bf16[16,4096]{1,0:T(8,128)(2,1)}, bf16[16,4096]{1,0:T(8,128)(2,1)}) custom-call(bf16[256,4096]{1,0:T(8,128)(2,1)} %get-tuple-element.16.x_ref, bf16[256,4096]{1,0:T(8,128)(2,1)} %get-tuple-element.17.g_ref, ...), custom_call_target="tpu_custom_call" | custom-call | tf_op jit(solution)/shard_map/weight_grads/pallas_call | solution.py:510

commit v3 on v2

--- a/solution.py
+++ b/solution.py
@@ -197,6 +197,7 @@
         arrived(0, 1, k)
         hop(0, 3, k).start()
     lax.fori_loop(cuts[2], cuts[3], mask_cat, 0)
+    lax.fori_loop(0, nj, mask_down, 0)
     gather_last(0)
 
     def h_send(j, k):
@@ -221,7 +222,6 @@
     lax.fori_loop(nj // 2, nj, hidden, 0)
     x_copy = pltpu.make_async_copy(x_all, x_out, o_sem.at[2])
     x_copy.start()
-    lax.fori_loop(0, nj, mask_down, 0)
 
     def act_send(j, k):
         at = act.at[own, lanes(j, BLK)]
@@ -240,7 +240,6 @@
             act_send(j, k).start()
         return carry
 
-    lax.fori_loop(0, nj, activate, 0)
     gather_last(1)
     g_copy = pltpu.make_async_copy(g_all, g_out, o_sem.at[3])
     g_copy.start()
@@ -262,6 +261,7 @@
         return carry
 
     lax.fori_loop(0, nj, back, 0)
+    lax.fori_loop(0, nj, activate, 0)
 
     def peer_rows(k):
         return pl.ds(pl.multiple_of(row_at(R - k) * half, half), half)
@@ -272,6 +272,27 @@
             remote(at, at, act_ss.at[k - 1, j], act_rs.at[k - 1, j], {"row": row_at(k)}).wait_recv()
         return carry
 
+    def gc_send(j, k):
+        at = gc.at[own, lanes(j, PAIR)]
+        return remote(at, at, gc_ss.at[k - 1, j], gc_rs.at[k - 1, j], {"row": row_at(k)})
+
+    def swiglu_back(j, carry):
+        cols = lanes(j, BLK)
+        grad = gf[own, cols]
+        for k in range(1, R):
+            ga_send(j, k).wait_recv()
+            grad = grad + gr[k - 1, :, cols].astype(F32)
+        both = hf[own, lanes(j, PAIR)]
+        gate, up = both[:, :BLK], both[:, BLK:]
+        sig = jax.nn.sigmoid(gate)
+        gg = (grad * up * sig * (1.0 + gate * (1.0 - sig))).astype(BF16)
+        gu = (grad * gate * sig).astype(BF16)
+        gc[own, lanes(j, PAIR)] = jnp.concatenate([gg, gu], axis=1)
+        for k in range(1, R):
+            gc_send(j, k).start()
+        return carry
+
+    lax.fori_loop(0, nj, swiglu_back, 0)
     lax.fori_loop(0, nj, act_wait, 0)
     act_copy = pltpu.make_async_copy(act, act_out, o_sem.at[4])
     act_copy.start()
@@ -348,27 +369,6 @@
             stage_b(0, q - 1)
     stage_b(0, NCH - 1)
 
-    def gc_send(j, k):
-        at = gc.at[own, lanes(j, PAIR)]
-        return remote(at, at, gc_ss.at[k - 1, j], gc_rs.at[k - 1, j], {"row": row_at(k)})
-
-    def swiglu_back(j, carry):
-        cols = lanes(j, BLK)
-        grad = gf[own, cols]
-        for k in range(1, R):
-            ga_send(j, k).wait_recv()
-            grad = grad + gr[k - 1, :, cols].astype(F32)
-        both = hf[own, lanes(j, PAIR)]
-        gate, up = both[:, :BLK], both[:, BLK:]
-        sig = jax.nn.sigmoid(gate)
-        gg = (grad * up * sig * (1.0 + gate * (1.0 - sig))).astype(BF16)
-        gu = (grad * gate * sig).astype(BF16)
-        gc[own, lanes(j, PAIR)] = jnp.concatenate([gg, gu], axis=1)
-        for k in range(1, R):
-            gc_send(j, k).start()
-        return carry
-
-    lax.fori_loop(0, nj, swiglu_back, 0)
     for q in range(NCH):
         stage_c(0, q)
 

time: 107 us -> 112 us (1.047)
  Pallas kernels: 106 us -> 111 us
    pallas_call x1, Pallas kernels: 93.4 us -> 98.6 us  [local(): pl.pallas_call(functools.partial(fused, R, C), out_shape=(S((rows, dl), B...]
where the time goes in v3:
time: 112 us
  Pallas kernels  111 us (99%)
    pallas_call x1, Pallas kernels, local(): pl.pallas_call(functools.partial(fused, R, C), out_shape=(S((rows, dl), B...  98.6 us
    pallas_call x1, Pallas kernels, local(): pl.pallas_call(weight_grads, grid=(dl // width,), out_shape=(S((dl, hid),...  12.7 us

profile of v3, /device:TPU:0, one launch (start us, length us, event | category | flops | bytes accessed | tf_op | source)
XLA Modules:
  0.0 112.0 jit_solution(9407054262833237729)
XLA Ops:
  0.6 98.6 %layer.1 = (bf16[16,4096]{1,0:T(8,128)(2,1)}, bf16[16,4096]{1,0:T(8,128)(2,1)}, bf16[256,4096]{1,0:T(8,128)(2,1)}, bf16[256,4096]{1,0:T(8,128)(2,1)}, bf16[256,8...) custom-call(bf16[16,4096]{1,0:T(8,128)(2,1)} %x_hbm.1, bf16[16,4096]{1,0:T(8,128)(2,1)} %g_hbm.1, bf16[4096,896]{1,0:T(8,128)(2,1)} %wg_hbm.1, ...), custom_call_target="tpu_custom_call" | custom-call | tf_op jit(solution)/shard_map/layer/pallas_call | solution.py:470
  99.3 12.7 %weight_grads.1 = (bf16[4096,896]{1,0:T(8,128)(2,1)}, bf16[4096,896]{1,0:T(8,128)(2,1)}, bf16[896,4096]{1,0:T(8,128)(2,1)}, bf16[16,4096]{1,0:T(8,128)(2,1)}, bf16[16,4096]{1,0:T(8,128)(2,1)}) custom-call(bf16[256,4096]{1,0:T(8,128)(2,1)} %get-tuple-element.16.x_ref, bf16[256,4096]{1,0:T(8,128)(2,1)} %get-tuple-element.17.g_ref, ...), custom_call_target="tpu_custom_call" | custom-call | tf_op jit(solution)/shard_map/weight_grads/pallas_call | solution.py:510
